TPU v7x, 128 devices: a whole 4x4x4 slice. The times are simulated.
128 devices in a mesh: dom: 64 (over x_hi, y, z, core), band: 2 (over x_lo).
Axes of the slice: x: 4 (x_hi: 2, x_lo: 2; x = x_hi * 2 + x_lo), y: 4, z: 4, core: 2. Of those that a mesh axis runs over, the one named last changes fastest.
Arguments:
- states: bfloat16 [1051392, 256], P('dom', 'band'), may hold values from -6 to 6
- mass_scale: float32 [1051392], P('dom'), may hold values from 0.5 to 2
- potential: float32 [64, 36864], P(None, 'dom'), may hold values from -6 to 6
- kinetic: bfloat16 [64, 64], replicated, may hold values from -0.75 to 0.75
- basis_fn: bfloat16 [64, 64], replicated, may hold values from -0.75 to 0.75
- connectivity: int32 [64, 36864], P(None, 'dom'), may hold values from 0 to 17796, as said below
- boundary: int32 [87616], P('dom'), may hold values from 0 to 16427, as said below
- owners: int32 [8, 8], replicated, may hold values from 0 to 63, as said below
Outputs:
- filtered: bfloat16 [1051392, 256], P('dom', 'band')
- projected: float32 [256, 2, 2, 1024], P('dom', 'band')
Inputs may be any that keep to these rules, and one draw needn't show every extreme that they name: `connectivity`: entries below 16428 are distinct owned nodes of the cell's domain; the others name the plane of the domain above. `boundary`: each domain's 1369 entries are distinct local node numbers. `owners`: in every column block of tiles no domain owns more than 4 tiles, and some domain owns exactly 4.
All inputs are finite; a program needn't handle non-finite values.
Results may differ from a plain program's by a relative error of at most 0.015.
Values may be sent and summed in bfloat16 or wider, within the bound.
No kernel may reach another device: no remote copies, remote signals or barrier semaphores. Data moves between devices by JAX's collectives and lax.ppermute only.
A program may use at most 128 MiB of HBM per device.

v0:
```python
import functools

import jax
import jax.numpy as jnp
from jax import lax
from jax.experimental import pallas as pl
from jax.experimental.pallas import tpu as pltpu
from jax.sharding import PartitionSpec as P

NPC = 64
QP = 64
TILE = 32
CAP = 4
CENTER = 1.0
INV_HALF = 0.25
EXACT = lax.Precision.HIGHEST
DIMS = (2, 4, 4, 2)

LANES = 128
ROWS = 128
GROUP = 4
TURN = 2 * GROUP
BATCH = 8
SCOPED = 24
WINDOW = 384
STRIDE = 1024
F32 = jnp.float32
BF16 = jnp.bfloat16
VMEM = pl.BlockSpec(memory_space=pltpu.VMEM)
SMEM = pl.BlockSpec(memory_space=pltpu.SMEM)
ANY = pl.BlockSpec(memory_space=pl.ANY)
HBM = pl.BlockSpec(memory_space=pltpu.HBM)


def round_up(count, unit):
    return -(-count // unit) * unit


def from_behind(value, axis, steps):
    count = lax.axis_size(axis)
    initial, last = (max(0, -steps), min(count, count - steps))
    return lax.ppermute(value, axis, [(source, source + steps) for source in range(initial, last)])


def params(mebibytes):
    return pltpu.CompilerParams(vmem_limit_bytes=mebibytes << 20)


def cost(us):
    return pl.CostEstimate(flops=us * 10**9, bytes_accessed=us * 10**6, transcendentals=0)


def by_rows(count, work):
    def step(i, _):
        work(pl.ds(pl.multiple_of(i * ROWS, ROWS), ROWS))
        return 0

    lax.fori_loop(0, count // ROWS, step, 0)


def by_entries(count, work):
    unroll = max(u for u in range(1, 65) if count % u == 0)

    def step(i, _):
        for j in range(unroll):
            work(i * unroll + j)
        return 0

    lax.fori_loop(0, count // unroll, step, 0)


def gather(src, lists, cells, out):
    for k, cell in enumerate(cells):
        for j in range(NPC):
            out[k * NPC + j : k * NPC + j + 1, :] = src[pl.ds(lists[j][cell], 1), :]


def multiply(vals, pot, base, stacked, basis_t, out):
    chunk = pl.multiple_of((base // LANES) * LANES, LANES)
    shift = lax.rem(LANES - lax.rem(base, LANES), LANES)
    columns = pltpu.roll(pot[:, pl.ds(chunk, LANES)], shift, 1)
    for p in range(0, GROUP, 2):
        pair = jnp.concatenate(
            [vals[k * NPC : (k + 1) * NPC, :] for k in (p, p + 1)], axis=1
        ).astype(BF16)
        both = jnp.dot(stacked, pair, preferred_element_type=F32)
        weight = jnp.concatenate(
            [jnp.broadcast_to(columns[:, k : k + 1], (QP, LANES)) for k in (p, p + 1)], axis=1
        )
        weighted = (weight * both[:QP]).astype(BF16)
        result = jnp.dot(basis_t, weighted, preferred_element_type=F32) + both[QP:]
        for k in (p, p + 1):
            out[k * NPC : (k + 1) * NPC, :] = result[:, (k - p) * LANES : (k - p + 1) * LANES]


def scatter(res, lists, cells, sums, batch):
    for p in range(0, GROUP, 2):
        for start in range(0, NPC, batch):
            moved = []
            for k in (p, p + 1):
                for j in range(start, start + batch):
                    row = pl.ds(lists[j][cells[k]], 1)
                    total = sums[k - p][row, :] + res[k * NPC + j : k * NPC + j + 1, :]
                    moved.append((k - p, row, total))
            for which, row, total in moved:
                sums[which][row, :] = total


def cells_of(group):
    return [group * GROUP + k for k in range(GROUP)]


def sweep(begin, end, repeated, src, lists, pot, stacked_ref, basis_t_ref, sums, vals, ress):
    def mult(slot, group, stacked, basis_t):
        multiply(vals[slot], pot, group * GROUP, stacked, basis_t, ress[slot])

    def two(i, _):
        first = 2 * i

        @pl.when(i >= 0)
        def _():
            scatter(ress[1], lists, cells_of(jnp.maximum(first - 1, 2 * begin)), sums, BATCH)
            mult(0, first, stacked_ref[...], basis_t_ref[...])
            gather(src, lists, cells_of(first + 1), vals[1])

        @pl.when(first >= 0)
        def _():
            scatter(ress[0], lists, cells_of(first), sums, BATCH)
            mult(1, first + 1, stacked_ref[...], basis_t_ref[...])
            gather(src, lists, cells_of(jnp.minimum(first + 2, 2 * end - 1)), vals[0])

        return 0

    @pl.when((end > begin) & (repeated == 0))
    def _():
        ress[1][...] = jnp.zeros_like(ress[1])
        gather(src, lists, cells_of(2 * begin), vals[0])
        lax.fori_loop(begin, end, two, 0)
        scatter(ress[1], lists, cells_of(2 * end - 1), sums, BATCH)

    @pl.when((end > begin) & (repeated != 0))
    def _():
        def one(i, _):
            gather(src, lists, cells_of(i), vals[0])
            mult(0, i, stacked_ref[...], basis_t_ref[...])
            scatter(ress[0], lists, cells_of(i), sums, 1)
            return 0

        lax.fori_loop(2 * begin, 2 * end, one, 0)


def start_kernel(edge_count, early, states, mass_rows, *refs):
    given, refs = refs[:early], refs[early:]
    mass, kept, states_edge, mass_edge, sent = refs[:5]
    held, wide, arrived = refs[5:10], refs[10], refs[11]
    edge = held[0]
    copies = [
        pltpu.make_async_copy(source, ref, arrived.at[n])
        for n, (source, ref) in enumerate(zip(given, held))
    ]
    for copy in copies:
        copy.start()
    nodes = states.shape[0]
    padded = kept.shape[0]
    whole = nodes // ROWS * ROWS

    def widen(rows):
        wide[rows, :] = states[rows, :].astype(F32)

    by_rows(whole, widen)
    if whole < padded:
        wide[whole:padded, :] = jnp.zeros((padded - whole, LANES), F32)
        wide[whole:nodes, :] = states[whole:nodes, :].astype(F32)

    def scale(columns, k, first):
        rows = pl.ds(pl.multiple_of(first + k * ROWS, ROWS), ROWS)
        column = jnp.broadcast_to(columns[:, k : k + 1], (ROWS, LANES))
        value = wide[rows, :]
        mass[rows, :] = column
        kept[rows, :] = value.astype(BF16)

    def eight(i, _):
        columns = mass_rows[pl.ds(pl.multiple_of(i * 8, 8), 8), :].T
        for k in range(8):
            scale(columns, k, i * (8 * ROWS))
        return 0

    chunks = padded // ROWS
    lax.fori_loop(0, chunks // 8, eight, 0)
    if chunks % 8:
        columns = mass_rows[chunks // 8 * 8 : chunks // 8 * 8 + 8, :].T
        for k in range(chunks % 8):
            scale(columns, k, chunks // 8 * 8 * ROWS)
    tail = states_edge.shape[0] - 8
    states_edge[tail:, :] = jnp.zeros((8, LANES), F32)
    mass_edge[tail:, :] = jnp.zeros((8, LANES), F32)

    for copy in copies:
        copy.wait()

    def take(i):
        row = pl.ds(edge[i], 1)
        states_edge[pl.ds(i, 1), :] = wide[row, :]
        mass_edge[pl.ds(i, 1), :] = mass[row, :]

    by_entries(edge_count, take)
    sent[...] = (mass_edge[...] * states_edge[...]).astype(BF16)


def cells_kernel(part, which, edge_count, padded, *refs):
    refs = list(refs)
    conn, counts, pot, stacked, basis_t = refs[:5]
    refs = refs[5:]
    first = part == 0 and which == 1
    if not first:
        src, sum_a, sum_b = refs[:3]
        refs = refs[3:]
    if part == 0 and which > 1:
        edge, scaled_edge = refs[:2]
        refs = refs[2:]
    if part == 1:
        ghost = refs.pop(0)
    sources = []
    if first:
        sources, refs = refs[:2], refs[2:]
    if part == 2:
        edge = refs.pop(0)
        if which == 3:
            second_edge = refs.pop(0)
        loads = 3 if which == 2 else 2
        sources, refs = refs[:loads], refs[loads:]
    if first:
        src, sum_a, sum_b = refs[:3]
    refs = refs[3:]
    if part == 1:
        outgoing = refs.pop(0)
    if part == 2:
        edge_sums, result = refs[:2]
        refs = refs[2:]
        if which == 3:
            second = refs.pop(0)
    val_a, val_b, res_a, res_b, arrived = refs[:5]
    lists, refs = refs[5 : 5 + NPC], refs[5 + NPC :]
    if first or part == 2:
        loaded, refs = refs[0], refs[1:]
        fetches = [
            pltpu.make_async_copy(source, ref, loaded.at[n])
            for n, (source, ref) in enumerate(zip(sources, refs))
        ]
    if first or part == 2:
        for fetch in fetches:
            fetch.start()
    split = counts[4] if which == 3 else counts[0]
    begin, end = ((0, split), (counts[1], counts[2]), (split, counts[1]))[part]
    slots = pot.shape[1]
    base = begin * TURN // LANES * LANES
    short = (end * TURN - base <= WINDOW) & (base + WINDOW <= slots)

    def list_copies(offset, size):
        return [
            pltpu.make_async_copy(
                conn.at[pl.ds(pl.multiple_of(offset + j * STRIDE, LANES), size)],
                lists[j].at[pl.ds(offset, size)],
                arrived.at[j],
            )
            for j in range(NPC)
        ]

    @pl.when(short)
    def _():
        for copy in list_copies(pl.multiple_of(base, LANES), WINDOW):
            copy.start()

    @pl.when(jnp.logical_not(short))
    def _():
        for copy in list_copies(0, slots):
            copy.start()

    if first:
        for fetch in fetches:
            fetch.wait()
        mass, values = refs

        def prepare(rows):
            scaled = (mass[rows, :] * values[rows, :].astype(F32)).astype(BF16)
            src[rows, :] = scaled.astype(F32)

        def clear(rows):
            sum_a[rows, :] = jnp.zeros((ROWS, LANES), F32)
            sum_b[rows, :] = jnp.zeros((ROWS, LANES), F32)

        by_rows(padded, prepare)
        by_rows(sum_a.shape[0], clear)
        src[padded:, :] = jnp.zeros((src.shape[0] - padded, LANES), F32)
    if part == 0 and which > 1:

        def patch(i):
            src[pl.ds(edge[i], 1), :] = scaled_edge[pl.ds(i, 1), :]

        by_entries(edge_count, patch)
    if part == 1:
        src[padded : padded + ghost.shape[0], :] = ghost[...].astype(F32)

    @pl.when(short)
    def _():
        for copy in list_copies(pl.multiple_of(base, LANES), WINDOW):
            copy.wait()

    @pl.when(jnp.logical_not(short))
    def _():
        for copy in list_copies(0, slots):
            copy.wait()

    sums = (sum_a, sum_b)
    sweep(
        begin,
        end,
        counts[3],
        src,
        lists,
        pot,
        stacked,
        basis_t,
        sums,
        (val_a, val_b),
        (res_a, res_b),
    )
    if part == 1:
        ghost_rows = slice(padded, padded + ghost.shape[0])
        outgoing[...] = (sum_a[ghost_rows, :] + sum_b[ghost_rows, :]).astype(BF16)
        blank = jnp.zeros(ghost.shape, F32)
        sum_a[ghost_rows, :] = blank
        sum_b[ghost_rows, :] = blank
    if part < 2:
        return

    for fetch in fetches:
        fetch.wait()
    mass, values = refs[:2]
    tail = edge_sums.shape[0] - 8
    edge_sums[tail:, :] = jnp.zeros((8, LANES), F32)

    def take(i):
        row = pl.ds(edge[i], 1)
        edge_sums[pl.ds(i, 1), :] = sum_a[row, :] + sum_b[row, :]
        if which == 3:
            sum_a[row, :] = jnp.zeros((1, LANES), F32)
            sum_b[row, :] = jnp.zeros((1, LANES), F32)

    by_entries(edge_count, take)

    def finish(rows):
        scale = mass[rows, :]
        image = scale * (sum_a[rows, :] + sum_b[rows, :])
        value = values[rows, :].astype(F32)
        if which == 3:
            refs[2][rows, :] = image.astype(BF16)
            src[rows, :] = value
            return
        if which == 1:
            after = ((image - CENTER * value) * INV_HALF).astype(BF16)
        else:
            start = refs[2][rows, :].astype(F32)
            after = (2.0 * INV_HALF * (image - CENTER * value) - start).astype(BF16)
        result[rows, :] = after
        src[rows, :] = (scale * after.astype(F32)).astype(BF16).astype(F32)
        sum_a[rows, :] = jnp.zeros((ROWS, LANES), F32)
        sum_b[rows, :] = jnp.zeros((ROWS, LANES), F32)

    by_rows(padded, finish)
    if which == 3:
        leaving = [
            pltpu.make_async_copy(refs[2], result.at[:, pl.ds(0, LANES)], loaded.at[0]),
            pltpu.make_async_copy(values, result.at[:, pl.ds(LANES, LANES)], loaded.at[1]),
        ]
        leaving[0].start()

        def blank(i):
            src[pl.ds(edge[i], 1), :] = jnp.zeros((1, LANES), F32)

        def fill(i):
            src[pl.ds(edge[i], 1), :] = second_edge[pl.ds(i, 1), :]

        def blanked(rows):
            values[rows, :] = src[rows, :].astype(BF16)

        def filled(rows):
            second[rows, :] = src[rows, :].astype(BF16)

        nodes = second.shape[0]
        by_entries(edge_count, blank)
        by_rows(padded, blanked)
        leaving[1].start()
        by_entries(edge_count, fill)
        whole = nodes // ROWS * ROWS
        by_rows(whole, filled)
        if whole < nodes:
            second[whole:nodes, :] = src[whole:nodes, :].astype(BF16)
        for copy in leaving:
            copy.wait()


def arrange(connectivity, potential, node_count, padded):
    cell_count = connectivity.shape[1]
    is_ghost = connectivity >= node_count
    late = jnp.any(is_ghost, axis=0).astype(F32)[None]
    before = jnp.triu(jnp.ones((cell_count, cell_count), F32), 1)
    ranks = jnp.dot(jnp.concatenate([late, 1.0 - late], 0), before, precision=EXACT)
    late_count = jnp.sum(late).astype(jnp.int32)
    turns = (cell_count - late_count + TURN - 1) // TURN
    late_turns = (late_count + TURN - 1) // TURN
    place = jnp.where(late[0] > 0, (turns * TURN).astype(F32) + ranks[0], ranks[1])
    slots = round_up(round_up(cell_count, TURN) + TURN, LANES)
    hot = (place[:, None] == jnp.arange(slots, dtype=F32)[None, :]).astype(F32)
    moved = jnp.dot(
        jnp.concatenate([connectivity.astype(F32), potential], 0), hot, precision=EXACT
    )
    index = jnp.round(moved[:NPC]).astype(jnp.int32)
    index = jnp.where(index >= node_count, index + (padded - node_count), index)
    used = jnp.sum(hot, axis=0) > 0
    spare = node_count + jnp.arange(NPC, dtype=jnp.int32)
    index = jnp.where(used[None, :], index, spare[:, None])
    lists = jnp.pad(index, ((0, 0), (0, STRIDE - slots))).reshape(-1)

    batched = jnp.where(is_ghost, connectivity, -1).reshape(NPC // BATCH, BATCH, cell_count)
    same = (batched[:, :, None] == batched[:, None, :]) & (batched[:, :, None] >= 0)
    apart = ~jnp.eye(BATCH, dtype=bool)[None, :, :, None]
    repeated = jnp.any(same & apart).astype(jnp.int32)
    counts = jnp.stack([turns // 2, turns, turns + late_turns, repeated, turns // 16])
    return lists, moved[NPC:], jnp.pad(counts, (0, LANES - counts.shape[0]))


def swap(value, dim, offset):
    step = 1
    for size in DIMS[dim + 1 :]:
        step *= size
    count, total = DIMS[dim], lax.axis_size("dom")
    pairs = []
    for source in range(total):
        digit = source // step % count
        pairs.append((source, source + ((digit + offset) % count - digit) * step))
    return lax.ppermute(value, "dom", pairs)


def choices(holder):
    here = lax.axis_index("dom")

    def digits(index):
        found = []
        for size in reversed(DIMS):
            found.append(index % size)
            index = index // size
        return found[::-1]

    mine, owner = digits(here), digits(holder)
    count = holder.shape[0]
    before = jnp.arange(count)[:, None] < jnp.arange(count)[None, :]

    def chosen(member, slots):
        rank = jnp.sum((member[:, None] & before).astype(jnp.int32), axis=0)
        return (member[None, :] & (rank[None, :] == jnp.arange(slots)[:, None])).astype(F32)

    column = (owner[0] == mine[0]) & (owner[3] == mine[3])
    plane_slots = min(count, DIMS[1] * CAP)
    for_plane = [
        chosen(column & (owner[2] == (mine[2] + k) % DIMS[2]), plane_slots)
        for k in range(DIMS[2])
    ]
    for_row = [
        chosen(column & (owner[2] == mine[2]) & (owner[1] == (mine[1] + k) % DIMS[1]), CAP)
        for k in range(DIMS[1])
    ]
    by_row = jnp.dot(jnp.concatenate(for_row, 0), for_plane[0].T, precision=EXACT)
    return jnp.concatenate(for_plane, 0), by_row


def to_owners(tiles, by_plane, by_row):
    plane_slots = by_row.shape[1]
    tiles = tiles + swap(tiles, 3, 1)
    tiles = tiles + swap(tiles.astype(BF16), 0, 1).astype(F32)
    parts = jnp.dot(by_plane, tiles, precision=EXACT)
    parts = parts.reshape(DIMS[2], plane_slots, tiles.shape[1])
    total = parts[0]
    for arrived in [swap(parts[k].astype(BF16), 2, k) for k in range(1, DIMS[2])]:
        total = total + arrived.astype(F32)
    parts = jnp.dot(by_row, total, precision=EXACT)
    parts = parts.reshape(DIMS[1], CAP, tiles.shape[1])
    total = parts[0]
    for arrived in [swap(parts[k].astype(BF16), 1, k) for k in range(1, DIMS[1])]:
        total = total + arrived.astype(F32)
    return total


def local(states, mass_scale, potential, kinetic, basis_fn, connectivity, boundary, owners):
    node_count, state_count = states.shape
    edge_count = boundary.shape[0]
    padded = round_up(node_count + NPC, ROWS)
    edge_rows = round_up(edge_count + 7, 16)
    total_rows = round_up(padded + edge_rows, ROWS)

    wide = pltpu.VMEM((total_rows, LANES), F32)
    edge_shape = jax.ShapeDtypeStruct((edge_rows, LANES), F32)
    edge_half = jax.ShapeDtypeStruct((edge_rows, LANES), BF16)
    near_sums = pltpu.VMEM((edge_rows, LANES), F32)
    near_half = pltpu.VMEM((edge_rows, LANES), BF16)
    padded_half = jax.ShapeDtypeStruct((padded, LANES), BF16)
    both_half = jax.ShapeDtypeStruct((padded, 2 * LANES), BF16)
    whole_half = jax.ShapeDtypeStruct((node_count, LANES), BF16)

    mass_count = round_up(padded, 8 * ROWS)
    mass_rows = jnp.pad(mass_scale, (0, mass_count - node_count)).reshape(mass_count // ROWS, ROWS)
    stacked = jnp.concatenate([basis_fn, kinetic], 0)
    basis_t = basis_fn.T
    lists, pot, counts = arrange(connectivity, potential, node_count, padded)
    boundary = jnp.pad(boundary, (0, round_up(edge_count, STRIDE) - edge_count))
    tile_rows = lax.axis_size("band") * state_count // TILE
    tile_cols = state_count // TILE
    tile_count = tile_rows * tile_cols
    holder = lax.dynamic_slice_in_dim(
        owners, lax.axis_index("band") * tile_cols, tile_cols, 1
    ).reshape(tile_count)
    by_plane, by_row = choices(holder)
    together = lax.ppermute(states[:16], "band", [(0, 1), (1, 0)])
    early = (boundary, counts, pot, stacked, basis_t, by_plane, by_row, together)
    mass, kept, states_edge, mass_edge, sent, *kept_small = pl.pallas_call(
        functools.partial(start_kernel, edge_count, len(early)),
        out_shape=(pltpu.HBM((padded, LANES), F32), pltpu.HBM((padded, LANES), BF16))
        + (edge_shape, edge_shape, edge_half)
        + tuple(pltpu.SMEM(given.shape, given.dtype) for given in early[:2])
        + tuple(pltpu.VMEM(given.shape, given.dtype) for given in early[2:5]),
        in_specs=[VMEM, VMEM] + [ANY] * len(early),
        out_specs=(VMEM,) * 5 + (SMEM,) * 2 + (VMEM,) * 3,
        scratch_shapes=[pltpu.VMEM((padded, LANES), F32), pltpu.SemaphoreType.DMA((5,))],
        compiler_params=params(SCOPED),
        cost_estimate=cost(10),
        name="start",
    )(states, mass_rows, *early)
    edge, counts, pot, stacked, basis_t = kept_small
    ghost = from_behind(sent, "dom", -1)
    block = pltpu.VMEM((GROUP * NPC, LANES), F32)

    def cells(part, which, held, specs, extra, outs, scratch=(), places=None):
        return pl.pallas_call(
            functools.partial(cells_kernel, part, which, edge_count, padded),
            out_shape=(wide, wide, wide) + outs,
            in_specs=[ANY, SMEM] + [VMEM] * (3 + len(held)) + specs,
            out_specs=(VMEM,) * 3 + (places or (VMEM,) * len(outs)),
            input_output_aliases={5: 0, 6: 1, 7: 2} if held else {},
            scratch_shapes=[block, block, block, block, pltpu.SemaphoreType.DMA((NPC,))]
            + [pltpu.SMEM((STRIDE,), jnp.int32)] * NPC
            + list(scratch),
            compiler_params=params(SCOPED),
            cost_estimate=cost(20),
            name=f"cells_{which}_{part}",
        )(lists, counts, pot, stacked, basis_t, *held, *extra)

    def joined(edge_sums, outgoing):
        incoming = from_behind(outgoing, "dom", 1)
        return mass_edge * (edge_sums + incoming.astype(F32))

    def scaled(edge):
        return (mass_edge * edge).astype(BF16)

    loaded = pltpu.SemaphoreType.DMA((3,))
    mass_room = pltpu.VMEM((padded, LANES), F32)
    half_room = pltpu.VMEM((padded, LANES), BF16)
    held = cells(0, 1, (), [HBM, HBM], (mass, kept), (), (loaded, mass_room, half_room))
    *held, outgoing = cells(1, 1, held, [VMEM], (ghost,), (near_half,))
    *held, sums, one = cells(
        2,
        1,
        held,
        [SMEM, HBM, HBM],
        (edge, mass, kept),
        (near_sums, padded_half),
        (loaded, mass_room, half_room),
    )
    one_edge = ((joined(sums, outgoing) - CENTER * states_edge) * INV_HALF).astype(BF16).astype(F32)

    sent = scaled(one_edge)
    ghost = from_behind(sent, "dom", -1)
    held = cells(0, 2, held, [SMEM, VMEM], (edge, sent.astype(F32)), ())
    *held, outgoing = cells(1, 2, held, [VMEM], (ghost,), (near_half,))
    *held, sums, two = cells(
        2,
        2,
        held,
        [SMEM, HBM, HBM, HBM],
        (edge, mass, one, kept),
        (near_sums, padded_half),
        (loaded, mass_room, half_room, half_room),
    )
    turned = [(0, 1), (1, 0)]
    two_half = (
        2.0 * INV_HALF * (joined(sums, outgoing) - CENTER * one_edge) - states_edge
    ).astype(BF16)
    two_edge = two_half.astype(F32)
    other_edge = lax.ppermute(two_half, "band", turned)

    sent = scaled(two_edge)
    ghost = from_behind(sent, "dom", -1)
    held = cells(0, 3, held, [SMEM, VMEM], (edge, sent.astype(F32)), ())
    ghost, two = lax.optimization_barrier((ghost, two))
    other = lax.ppermute(two, "band", turned)
    *held, outgoing = cells(1, 3, held, [VMEM], (ghost,), (near_half,))
    *held, sums, own, second = cells(
        2,
        3,
        held,
        [SMEM, VMEM, HBM, HBM],
        (edge, two_edge, mass, two),
        (near_sums, both_half, whole_half),
        (loaded, mass_room, half_room, half_room),
        (VMEM, ANY, VMEM),
    )
    image_edge = joined(sums, outgoing).astype(BF16)
    own_edge = jnp.concatenate([image_edge, two_half], 1)

    def project(columns, mine):
        return lax.dot_general(
            columns, mine, (((0,), (0,)), ((), ())), preferred_element_type=F32
        )

    inverse = 1.0 / (node_count * lax.axis_size("dom"))
    near_own, near_edge = lax.optimization_barrier((own, own_edge))
    near = (project(two, near_own) + project(two_half, near_edge)) * inverse
    far = (project(other, own) + project(other_edge, own_edge)) * inverse
    lower = lax.axis_index("band") == 0
    pair = jnp.concatenate([jnp.where(lower, near, far), jnp.where(lower, far, near)], 0)

    tile_vals = (
        pair.reshape(tile_rows, TILE, 2, tile_cols, TILE)
        .transpose(0, 3, 2, 1, 4)
        .reshape(tile_count, 2 * TILE * TILE)
    )
    mine = to_owners(tile_vals, by_plane, by_row)
    return (second, mine.reshape(CAP, 1, 2, TILE * TILE))


def solution(mesh):
    return jax.shard_map(
        local,
        mesh=mesh,
        in_specs=(
            P("dom", "band"),
            P("dom"),
            P(None, "dom"),
            P(),
            P(),
            P(None, "dom"),
            P("dom"),
            P(),
        ),
        out_specs=(P("dom", "band"), P("dom", "band", None, None)),
        check_vma=False,
    )
```

profile of v0, /device:TPU:0, one launch (start us, length us, event | category | flops | bytes accessed | tf_op | source)
XLA Modules:
  0.0 355.6 jit_solution(9822633369615544107)
XLA Ops:
  0.6 0.7 slice.57
  1.3 1.6 collective-permute-start
  2.9 0.9 compare_reduce_fusion
  3.9 0.6 convert_reduce_fusion.9
  5.1 1.0 fusion.18
  6.2 1.0 broadcast_compare_fusion
  8.4 0.9 pad_bitcast_fusion.1.mass_rows
  9.3 0.5 fusion.1
  10.1 1.7 fusion
  11.9 0.7 pad_maximum_fusion.2.refs_3_
  12.7 1.1 and_reduce_fusion
  14.0 0.8 copy.39
  15.6 0.7 pad.18.refs_0_
  16.3 2.2 copy-done.2
  18.5 13.0 %start.1 = (f32[16512,128]{1,0:T(8,128)}, bf16[16512,128]{1,0:T(8,128)(2,1)}, f32[1376,128]{1,0:T(8,128)S(1)}, f32[1376,128]{1,0:T(8,128)S(1)}, bf16[1376,128]{1...) custom-call(bf16[16428,128]{1,0:T(8,128)(2,1)S(1)} %copy-done.2, ...), custom_call_target="tpu_custom_call" | custom-call | flops 10000000000 | bytes 10000000 | tf_op jit(solution)/shard_map/start/pallas_call | solution.py:525
  31.5 1.3 collective-permute-start.1
  32.8 31.2 %cells_1_0.1 = (f32[17920,128]{1,0:T(8,128)S(1)}, f32[17920,128]{1,0:T(8,128)S(1)}, f32[17920,128]{1,0:T(8,128)S(1)}) custom-call(s32[65536]{0:T(1024)S(1)} %bitcast.29, s32[128]{0:T(128)S(4)} %get-tuple-element.50.refs_1_, f32[64,640]{1,0:T(8,128)S(1)} %get-tuple-element.51.refs_2_, bf16[128,64]{1,0:T(8,128)(2,1)S(1)} %get-tuple-element.52.refs_3_, ...), custom_call_target="tpu_custom_call" | custom-call | flops 20000000000 | bytes 20000000 | tf_op jit(solution)/shard_map/cells_1_0/pallas_call | solution.py:543
  64.1 19.0 %cells_1_1.1 = (f32[17920,128]{1,0:T(8,128)S(1)}, f32[17920,128]{1,0:T(8,128)S(1)}, f32[17920,128]{1,0:T(8,128)S(1)}, bf16[1376,128]{1,0:T(8,128)(2,1)S(1)}) custom-call(s32[65536]{0:T(1024)S(1)} %bitcast.30, s32[128]{0:T(128)S(4)} %get-tuple-element.50.refs_1_, ...), custom_call_target="tpu_custom_call", output_to_operand_aliasing={{0}: (5, {}), {1}: (6, {}), {2}: (7, {})} | custom-call | flops 20000000000 | bytes 20000000 | tf_op jit(solution)/shard_map/cells_1_1/pallas_call | solution.py:543
  83.1 3.0 collective-permute-start.2
  86.2 32.4 %cells_1_2.1 = (f32[17920,128]{1,0:T(8,128)S(1)}, f32[17920,128]{1,0:T(8,128)S(1)}, f32[17920,128]{1,0:T(8,128)S(1)}, f32[1376,128]{1,0:T(8,128)S(1)}, bf16[16512,128]{1,0:T(8,128)(2,1)}) custom-call(s32[65536]{0:T(1024)S(1)} %bitcast.31, s32[128]{0:T(128)S(4)} %get-tuple-element.50.refs_1_, ...), custom_call_target="tpu_custom_call", output_to_operand_aliasing={{0}: (5, {}), {1}: (6, {}), {2}: (7, {})} | custom-call | flops 20000000000 | bytes 20000000 | tf_op jit(solution)/shard_map/cells_1_2/pallas_call | solution.py:543
  118.8 1.3 collective-permute-start.3
  120.1 25.6 %cells_2_0.1 = (f32[17920,128]{1,0:T(8,128)S(1)}, f32[17920,128]{1,0:T(8,128)S(1)}, f32[17920,128]{1,0:T(8,128)S(1)}) custom-call(s32[65536]{0:T(1024)S(1)} %bitcast.32, s32[128]{0:T(128)S(4)} %get-tuple-element.50.refs_1_, f32[64,640]{1,0:T(8,128)S(1)} %get-tuple-element.51.refs_2_, ...), custom_call_target="tpu_custom_call", output_to_operand_aliasing={{0}: (5, {}), {1}: (6, {}), {2}: (7, {})} | custom-call | flops 20000000000 | bytes 20000000 | tf_op jit(solution)/shard_map/cells_2_0/pallas_call | solution.py:543
  145.8 19.0 %cells_2_1.1 = (f32[17920,128]{1,0:T(8,128)S(1)}, f32[17920,128]{1,0:T(8,128)S(1)}, f32[17920,128]{1,0:T(8,128)S(1)}, bf16[1376,128]{1,0:T(8,128)(2,1)S(1)}) custom-call(s32[65536]{0:T(1024)S(1)} %bitcast.33, s32[128]{0:T(128)S(4)} %get-tuple-element.50.refs_1_, ...), custom_call_target="tpu_custom_call", output_to_operand_aliasing={{0}: (5, {}), {1}: (6, {}), {2}: (7, {})} | custom-call | flops 20000000000 | bytes 20000000 | tf_op jit(solution)/shard_map/cells_2_1/pallas_call | solution.py:543
  164.8 4.0 %collective-permute-start.4 = (bf16[1376,128]{1,0:T(8,128)(2,1)S(1)}, bf16[1376,128]{1,0:T(8,128)(2,1)S(1)}, u32[]{:S(2)}, u32[]{:S(2)}) collective-permute-start(bf16[1376,128]{1,0:T(8,128)(2,1)S(1)} %get-tuple-element.82), channel_id=1, source_target_pairs={{0,2},{2,4},{4,6},{6,8},{8,10},{10,12},{12,14},{14,16},{16,18},{18... | collective-permute-start | bytes 1056776 | tf_op jit(solution)/shard_map/ppermute | solution.py:42
  168.8 32.9 %cells_2_2.1 = (f32[17920,128]{1,0:T(8,128)S(1)}, f32[17920,128]{1,0:T(8,128)S(1)}, f32[17920,128]{1,0:T(8,128)S(1)}, f32[1376,128]{1,0:T(8,128)S(1)}, bf16[16512,128]{1,0:T(8,128)(2,1)}) custom-call(s32[65536]{0:T(1024)S(1)} %bitcast.34, s32[128]{0:T(128)S(4)} %get-tuple-element.50.refs_1_, ...), custom_call_target="tpu_custom_call", output_to_operand_aliasing={{0}: (5, {}), {1}: (6, {}), {2}: (7, {})} | custom-call | flops 20000000000 | bytes 20000000 | tf_op jit(solution)/shard_map/cells_2_2/pallas_call | solution.py:543
  202.1 0.6 collective-permute-start.8
  202.8 1.3 collective-permute-start.5
  204.0 5.6 %cells_3_0.1 = (f32[17920,128]{1,0:T(8,128)S(1)}, f32[17920,128]{1,0:T(8,128)S(1)}, f32[17920,128]{1,0:T(8,128)S(1)}) custom-call(s32[65536]{0:T(1024)S(1)} %bitcast.35, s32[128]{0:T(128)S(4)} %get-tuple-element.50.refs_1_, f32[64,640]{1,0:T(8,128)S(1)} %get-tuple-element.51.refs_2_, ...), custom_call_target="tpu_custom_call", output_to_operand_aliasing={{0}: (5, {}), {1}: (6, {}), {2}: (7, {})} | custom-call | flops 20000000000 | bytes 20000000 | tf_op jit(solution)/shard_map/cells_3_0/pallas_call | solution.py:543
  209.7 1.6 collective-permute-start.7
  211.2 19.0 %cells_3_1.1 = (f32[17920,128]{1,0:T(8,128)S(1)}, f32[17920,128]{1,0:T(8,128)S(1)}, f32[17920,128]{1,0:T(8,128)S(1)}, bf16[1376,128]{1,0:T(8,128)(2,1)S(1)}) custom-call(s32[65536]{0:T(1024)S(1)} %bitcast.36, s32[128]{0:T(128)S(4)} %get-tuple-element.50.refs_1_, ...), custom_call_target="tpu_custom_call", output_to_operand_aliasing={{0}: (5, {}), {1}: (6, {}), {2}: (7, {})} | custom-call | flops 20000000000 | bytes 20000000 | tf_op jit(solution)/shard_map/cells_3_1/pallas_call | solution.py:543
  230.3 4.7 %collective-permute-start.6 = (bf16[1376,128]{1,0:T(8,128)(2,1)S(1)}, bf16[1376,128]{1,0:T(8,128)(2,1)S(1)}, u32[]{:S(2)}, u32[]{:S(2)}) collective-permute-start(bf16[1376,128]{1,0:T(8,128)(2,1)S(1)} %get-tuple-element.95), channel_id=1, source_target_pairs={{0,2},{2,4},{4,6},{6,8},{8,10},{10,12},{12,14},{14,16},{16,18},{18... | collective-permute-start | bytes 1056776 | tf_op jit(solution)/shard_map/ppermute | solution.py:42
  235.0 60.0 %cells_3_2.1 = (f32[17920,128]{1,0:T(8,128)S(1)}, f32[17920,128]{1,0:T(8,128)S(1)}, f32[17920,128]{1,0:T(8,128)S(1)}, f32[1376,128]{1,0:T(8,128)S(1)}, bf16[1651...) custom-call(s32[65536]{0:T(1024)S(1)} %bitcast.37, ...), custom_call_target="tpu_custom_call", output_to_operand_aliasing={{0}: (5, {}), {1}: (6, {}), {2}: (7, {})} | custom-call | flops 20000000000 | bytes 20000000 | tf_op jit(solution)/shard_map/cells_3_2/pallas_call | solution.py:543
  295.9 6.1 %collective-permute-done.7 = bf16[16512,128]{1,0:T(8,128)(2,1)S(1)} collective-permute-done((bf16[16512,128]{1,0:T(8,128)(2,1)}, bf16[16512,128]{1,0:T(8,128)(2,1)S(1)}, u32[]{:S(2)}, u32[]{:S(2)}) %collective-permute-start.7) | collective-permute-done | bytes 4227104 | tf_op jit(solution)/shard_map/ppermute | solution.py:604
  301.9 5.2 %fusion.3 = f32[128,256]{1,0:T(8,128)S(1)} fusion(f32[128,256]{1,0:T(8,128)S(1)} %fusion.67, bf16[16512,128]{1,0:T(8,128)(2,1)S(1)} %collective-permute-done.7, bf16[16512,256]{1,0:T(8,128)(2,1)} %get-tuple-element.96), kind=kOutput, calls=%fused_computation.8 | convolution fusion | flops 1082195968 | bytes 12943360 | tf_op jit(solution)/shard_map/dot_general | solution.py:620
  307.2 1.5 broadcast_select_fusion.1
  309.4 0.5 reshape.584
  309.9 2.1 collective-permute-start.9
  312.0 1.2 collective-permute-done.9
  313.2 24.0 %collective-permute-start.10 = (bf16[32,2048]{1,0:T(8,128)(2,1)S(1)}, bf16[32,2048]{1,0:T(8,128)(2,1)S(1)}, u32[]{:S(2)}, u32[]{:S(2)}) collective-permute-start(bf16[32,2048]{1,0:T(8,128)(2,1)S(1)} %get-tuple-element.106), channel_id=1, source_target_pairs={{0,64},{2,66},{4,68},{6,70},{8,72},{10,74},{12,76},{14,78},{16,80}... | collective-permute-start | bytes 393224 | tf_op jit(solution)/shard_map/ppermute | solution.py:442
  337.2 3.8 %collective-permute-done.10 = bf16[32,2048]{1,0:T(8,128)(2,1)S(1)} collective-permute-done((bf16[32,2048]{1,0:T(8,128)(2,1)S(1)}, bf16[32,2048]{1,0:T(8,128)(2,1)S(1)}, u32[]{:S(2)}, u32[]{:S(2)}) %collective-permute-start.10) | collective-permute-done | bytes 131104 | tf_op jit(solution)/shard_map/ppermute | solution.py:442
  341.6 3.1 collective-permute-start.13
  344.8 3.0 collective-permute-done.11
  347.8 0.8 collective-permute-done.13
  348.9 1.2 collective-permute-start.15
  350.2 2.0 collective-permute-start.16
  352.2 1.7 collective-permute-done.14
  354.3 0.6 collective-permute-done.16
  354.9 0.7 reshape.585
  (100 shorter events, 5.2 us)
Async XLA Ops:
  0.6 6.6 %copy-start = (s32[8,8]{1,0:T(8,128)S(1)}, s32[8,8]{1,0:T(8,128)}, u32[]{:S(2)}) copy-start(s32[8,8]{1,0:T(8,128)} %param.15) | copy-start | bytes 772
  1.3 15.0 %collective-permute-start = (bf16[16,128]{1,0:T(8,128)(2,1)S(1)}, bf16[16,128]{1,0:T(8,128)(2,1)S(1)}, u32[]{:S(2)}, u32[]{:S(2)}) collective-permute-start(bf16[16,128]{1,0:T(8,128)(2,1)S(1)} %slice.57), channel_id=1, source_target_pairs={{0,1},{1,0},{2,3},{3,2},{4,5},{5,4},{6,7},{7,6},{8,9},{9,8},{10,11... | collective-permute-start | bytes 12296 | tf_op jit(solution)/shard_map/ppermute | solution.py:523
  8.0 7.4 %copy-start.3 = (pred[16,32]{1,0:T(8,128)(4,1)}, pred[16,32]{1,0:T(8,128)(4,1)S(1)}, u32[]{:S(2)}) copy-start(pred[16,32]{1,0:T(8,128)(4,1)S(1)} %fusion.38) | copy-start | bytes 1540
  8.1 23.4 %copy-start.5 = (pred[16,32]{1,0:T(8,128)(4,1)}, pred[16,32]{1,0:T(8,128)(4,1)S(1)}, u32[]{:S(2)}) copy-start(pred[16,32]{1,0:T(8,128)(4,1)S(1)} %fusion.39) | copy-start | bytes 1540
  8.2 23.3 %copy-start.7 = (pred[16,32]{1,0:T(8,128)(4,1)}, pred[16,32]{1,0:T(8,128)(4,1)S(1)}, u32[]{:S(2)}) copy-start(pred[16,32]{1,0:T(8,128)(4,1)S(1)} %fusion.40) | copy-start | bytes 1540
  8.3 23.2 %copy-start.9 = (pred[16,32]{1,0:T(8,128)(4,1)}, pred[16,32]{1,0:T(8,128)(4,1)S(1)}, u32[]{:S(2)}) copy-start(pred[16,32]{1,0:T(8,128)(4,1)S(1)} %fusion.41) | copy-start | bytes 1540
  16.3 2.2 copy-start.2
  31.5 32.5 %collective-permute-start.1 = (bf16[1376,128]{1,0:T(8,128)(2,1)S(1)}, bf16[1376,128]{1,0:T(8,128)(2,1)S(1)}, u32[]{:S(2)}, u32[]{:S(2)}) collective-permute-start(bf16[1376,128]{1,0:T(8,128)(2,1)S(1)} %get-tuple-element.59), channel_id=1, source_target_pairs={{2,0},{4,2},{6,4},{8,6},{10,8},{12,10},{14,12},{16,14},{18,16},{20... | collective-permute-start | bytes 1056776 | tf_op jit(solution)/shard_map/ppermute | solution.py:42
  83.1 35.5 %collective-permute-start.2 = (bf16[1376,128]{1,0:T(8,128)(2,1)S(1)}, bf16[1376,128]{1,0:T(8,128)(2,1)S(1)}, u32[]{:S(2)}, u32[]{:S(2)}) collective-permute-start(bf16[1376,128]{1,0:T(8,128)(2,1)S(1)} %get-tuple-element.69), channel_id=1, source_target_pairs={{0,2},{2,4},{4,6},{6,8},{8,10},{10,12},{12,14},{14,16},{16,18},{18... | collective-permute-start | bytes 1056776 | tf_op jit(solution)/shard_map/ppermute | solution.py:42
  118.8 26.9 %collective-permute-start.3 = (bf16[1376,128]{1,0:T(8,128)(2,1)S(1)}, bf16[1376,128]{1,0:T(8,128)(2,1)S(1)}, u32[]{:S(2)}, u32[]{:S(2)}) collective-permute-start(bf16[1376,128]{1,0:T(8,128)(2,1)S(1)} %get-tuple-element.113), channel_id=1, source_target_pairs={{2,0},{4,2},{6,4},{8,6},{10,8},{12,10},{14,12},{16,14},{18,16},{20... | collective-permute-start | bytes 1056776 | tf_op jit(solution)/shard_map/ppermute | solution.py:42
  164.8 36.9 %collective-permute-start.4 = (bf16[1376,128]{1,0:T(8,128)(2,1)S(1)}, bf16[1376,128]{1,0:T(8,128)(2,1)S(1)}, u32[]{:S(2)}, u32[]{:S(2)}) collective-permute-start(bf16[1376,128]{1,0:T(8,128)(2,1)S(1)} %get-tuple-element.82), channel_id=1, source_target_pairs={{0,2},{2,4},{4,6},{6,8},{8,10},{10,12},{12,14},{14,16},{16,18},{18... | collective-permute-start | bytes 1056776 | tf_op jit(solution)/shard_map/ppermute | solution.py:42
  202.1 93.0 %collective-permute-start.8 = (bf16[1376,128]{1,0:T(8,128)(2,1)S(1)}, bf16[1376,128]{1,0:T(8,128)(2,1)S(1)}, u32[]{:S(2)}, u32[]{:S(2)}) collective-permute-start(bf16[1376,128]{1,0:T(8,128)(2,1)S(1)} %get-tuple-element.109), channel_id=1, source_target_pairs={{0,1},{1,0},{2,3},{3,2},{4,5},{5,4},{6,7},{7,6},{8,9},{9,8},{10,11... | collective-permute-start | bytes 1056776 | tf_op jit(solution)/shard_map/ppermute | solution.py:598
  202.8 6.9 %collective-permute-start.5 = (bf16[1376,128]{1,0:T(8,128)(2,1)S(1)}, bf16[1376,128]{1,0:T(8,128)(2,1)S(1)}, u32[]{:S(2)}, u32[]{:S(2)}) collective-permute-start(bf16[1376,128]{1,0:T(8,128)(2,1)S(1)} %get-tuple-element.111), channel_id=1, source_target_pairs={{2,0},{4,2},{6,4},{8,6},{10,8},{12,10},{14,12},{16,14},{18,16},{20... | collective-permute-start | bytes 1056776 | tf_op jit(solution)/shard_map/ppermute | solution.py:42
  209.7 92.3 %collective-permute-start.7 = (bf16[16512,128]{1,0:T(8,128)(2,1)}, bf16[16512,128]{1,0:T(8,128)(2,1)S(1)}, u32[]{:S(2)}, u32[]{:S(2)}) collective-permute-start(bf16[16512,128]{1,0:T(8,128)(2,1)} %get-tuple-element.91.refs_11_), channel_id=1, source_target_pairs={{0,1},{1,0},{2,3},{3,2},{4,5},{5,4},{6,7},{7,6},{8,9},{9,8},{10,11... | collective-permute-start | bytes 12681224 | tf_op jit(solution)/shard_map/ppermute | solution.py:604
  230.3 64.7 %collective-permute-start.6 = (bf16[1376,128]{1,0:T(8,128)(2,1)S(1)}, bf16[1376,128]{1,0:T(8,128)(2,1)S(1)}, u32[]{:S(2)}, u32[]{:S(2)}) collective-permute-start(bf16[1376,128]{1,0:T(8,128)(2,1)S(1)} %get-tuple-element.95), channel_id=1, source_target_pairs={{0,2},{2,4},{4,6},{6,8},{8,10},{10,12},{12,14},{14,16},{16,18},{18... | collective-permute-start | bytes 1056776 | tf_op jit(solution)/shard_map/ppermute | solution.py:42
  295.5 11.6 %slice-start = ((s8[8454144]{0:T(1024)(128)(4,1)}), s8[4194304]{0:T(1024)(128)(4,1)S(1)}, s32[]{:S(2)}) async-start(s8[8454144]{0:T(1024)(128)(4,1)} %bitcast.39), calls=%async_computation | async-start | bytes 8388608
  295.5 11.6 %slice-start.3 = ((s8[4227072]{0:T(1024)(128)(4,1)}), s8[4194304]{0:T(1024)(128)(4,1)S(1)}, s32[]{:S(2)}) async-start(s8[4227072]{0:T(1024)(128)(4,1)} %bitcast.41), calls=%async_computation.3 | async-start | bytes 8388608
  295.8 11.3 %slice-start.1 = ((s8[8454144]{0:T(1024)(128)(4,1)}), s8[4194304]{0:T(1024)(128)(4,1)S(1)}, s32[]{:S(2)}) async-start(s8[8454144]{0:T(1024)(128)(4,1)} %bitcast.39), calls=%async_computation.1 | async-start | bytes 8388608
  295.8 11.3 %slice-start.2 = ((s8[8454144]{0:T(1024)(128)(4,1)}), s8[65536]{0:T(1024)(128)(4,1)S(1)}, s32[]{:S(2)}) async-start(s8[8454144]{0:T(1024)(128)(4,1)} %bitcast.39), calls=%async_computation.2 | async-start | bytes 131072
  295.9 11.3 %slice-start.4 = ((s8[4227072]{0:T(1024)(128)(4,1)}), s8[32768]{0:T(1024)(128)(4,1)S(1)}, s32[]{:S(2)}) async-start(s8[4227072]{0:T(1024)(128)(4,1)} %bitcast.41), calls=%async_computation.4 | async-start | bytes 65536
  307.2 33.9 %copy-start.4 = (pred[16,32]{1,0:T(8,128)(4,1)S(1)}, pred[16,32]{1,0:T(8,128)(4,1)}, u32[]{:S(2)}) copy-start(pred[16,32]{1,0:T(8,128)(4,1)} %copy-done.3) | copy-start | bytes 1540
  307.2 33.9 %copy-start.6 = (pred[16,32]{1,0:T(8,128)(4,1)S(1)}, pred[16,32]{1,0:T(8,128)(4,1)}, u32[]{:S(2)}) copy-start(pred[16,32]{1,0:T(8,128)(4,1)} %copy-done.5) | copy-start | bytes 1540
  307.2 33.9 %copy-start.8 = (pred[16,32]{1,0:T(8,128)(4,1)S(1)}, pred[16,32]{1,0:T(8,128)(4,1)}, u32[]{:S(2)}) copy-start(pred[16,32]{1,0:T(8,128)(4,1)} %copy-done.7) | copy-start | bytes 1540
  307.2 33.9 %copy-start.10 = (pred[16,32]{1,0:T(8,128)(4,1)S(1)}, pred[16,32]{1,0:T(8,128)(4,1)}, u32[]{:S(2)}) copy-start(pred[16,32]{1,0:T(8,128)(4,1)} %copy-done.9) | copy-start | bytes 1540
  307.2 48.4 %copy-start.1 = (s32[8,8]{1,0:T(8,128)S(1)}, s32[8,8]{1,0:T(8,128)}, u32[]{:S(2)}) copy-start(s32[8,8]{1,0:T(8,128)} %param.15) | copy-start | bytes 772
  309.9 3.2 collective-permute-start.9
  313.2 27.8 %collective-permute-start.10 = (bf16[32,2048]{1,0:T(8,128)(2,1)S(1)}, bf16[32,2048]{1,0:T(8,128)(2,1)S(1)}, u32[]{:S(2)}, u32[]{:S(2)}) collective-permute-start(bf16[32,2048]{1,0:T(8,128)(2,1)S(1)} %get-tuple-element.106), channel_id=1, source_target_pairs={{0,64},{2,66},{4,68},{6,70},{8,72},{10,74},{12,76},{14,78},{16,80}... | collective-permute-start | bytes 393224 | tf_op jit(solution)/shard_map/ppermute | solution.py:442
  341.5 6.3 %collective-permute-start.11 = (bf16[16,2048]{1,0:T(8,128)(2,1)S(1)}, bf16[16,2048]{1,0:T(8,128)(2,1)S(1)}, u32[]{:S(2)}, u32[]{:S(2)}) collective-permute-start(bf16[16,2048]{1,0:T(8,128)(2,1)S(1)} %get-tuple-element.121), channel_id=1, source_target_pairs={{0,4},{2,6},{4,8},{6,10},{8,12},{10,14},{12,0},{14,2},{16,20},{18,... | collective-permute-start | bytes 196616 | tf_op jit(solution)/shard_map/ppermute | solution.py:442
  341.5 6.2 %collective-permute-start.12 = (bf16[16,2048]{1,0:T(8,128)(2,1)S(1)}, bf16[16,2048]{1,0:T(8,128)(2,1)S(1)}, u32[]{:S(2)}, u32[]{:S(2)}) collective-permute-start(bf16[16,2048]{1,0:T(8,128)(2,1)S(1)} %get-tuple-element.123), channel_id=1, source_target_pairs={{0,8},{2,10},{4,12},{6,14},{8,0},{10,2},{12,4},{14,6},{16,24},{18,... | collective-permute-start | bytes 196616 | tf_op jit(solution)/shard_map/ppermute | solution.py:442
  341.6 6.9 %collective-permute-start.13 = (bf16[16,2048]{1,0:T(8,128)(2,1)S(1)}, bf16[16,2048]{1,0:T(8,128)(2,1)S(1)}, u32[]{:S(2)}, u32[]{:S(2)}) collective-permute-start(bf16[16,2048]{1,0:T(8,128)(2,1)S(1)} %get-tuple-element.122), channel_id=1, source_target_pairs={{0,12},{2,14},{4,0},{6,2},{8,4},{10,6},{12,8},{14,10},{16,28},{18,... | collective-permute-start | bytes 196616 | tf_op jit(solution)/shard_map/ppermute | solution.py:442
  348.9 5.0 %collective-permute-start.14 = (bf16[4,2048]{1,0:T(4,128)(2,1)S(1)}, bf16[4,2048]{1,0:T(4,128)(2,1)S(1)}, u32[]{:S(2)}, u32[]{:S(2)}) collective-permute-start(bf16[4,2048]{1,0:T(4,128)(2,1)S(1)} %get-tuple-element.128), channel_id=1, source_target_pairs={{0,16},{2,18},{4,20},{6,22},{8,24},{10,26},{12,28},{14,30},{16,32}... | collective-permute-start | bytes 49160 | tf_op jit(solution)/shard_map/ppermute | solution.py:442
  348.9 5.3 %collective-permute-start.15 = (bf16[4,2048]{1,0:T(4,128)(2,1)S(1)}, bf16[4,2048]{1,0:T(4,128)(2,1)S(1)}, u32[]{:S(2)}, u32[]{:S(2)}) collective-permute-start(bf16[4,2048]{1,0:T(4,128)(2,1)S(1)} %get-tuple-element.130), channel_id=1, source_target_pairs={{0,32},{2,34},{4,36},{6,38},{8,40},{10,42},{12,44},{14,46},{16,48}... | collective-permute-start | bytes 49160 | tf_op jit(solution)/shard_map/ppermute | solution.py:442
  350.2 4.7 %collective-permute-start.16 = (bf16[4,2048]{1,0:T(4,128)(2,1)S(1)}, bf16[4,2048]{1,0:T(4,128)(2,1)S(1)}, u32[]{:S(2)}, u32[]{:S(2)}) collective-permute-start(bf16[4,2048]{1,0:T(4,128)(2,1)S(1)} %get-tuple-element.129), channel_id=1, source_target_pairs={{0,48},{2,50},{4,52},{6,54},{8,56},{10,58},{12,60},{14,62},{16,0},... | collective-permute-start | bytes 49160 | tf_op jit(solution)/shard_map/ppermute | solution.py:442
where the time goes:
time: 357 us; the launch traced here: 356 us
  Pallas kernels  258 us (72%)
  starting transfers between devices  52.1 us (15%)
  waiting for transfers between devices  17.6 us (5%)
  matrix products  10.3 us (3%)
  local copies, waits for them, and re-layouts  7.52 us (2%)
  other arithmetic  7.5 us (2%)
    pallas_call x9, Pallas kernels, cells(): pl.pallas_call(functools.partial(cells_kernel, part, which, edge_count, p...  245 us
    ppermute x8, starting transfers between devices, swap(): return lax.ppermute(value, 'dom', pairs)  32.7 us
    ppermute x6, starting transfers between devices, from_behind(): lax.ppermute(value, axis, [(source, source + steps) for source in range(i...  15.7 us
    pallas_call x1, Pallas kernels, local(): pl.pallas_call(functools.partial(start_kernel, edge_count, len(early)), o...  13 us
    ppermute x8, waiting for transfers between devices, swap(): return lax.ppermute(value, 'dom', pairs)  11.5 us
    dot_general x4, matrix products, project(): lax.dot_general(columns, mine, (((0,), (0,)), ((), ())), preferred_elemen...  7.3 us
  transfers between devices with their start and end apart: 17, of which 8 were waited for; matrix products, arithmetic and copies ran while one was open for 4% of the time, Pallas kernels for 58%

commit v1 on v0

--- a/solution.py
+++ b/solution.py
@@ -22,7 +22,7 @@
 TURN = 2 * GROUP
 BATCH = 8
 SCOPED = 24
-WINDOW = 384
+WINDOWS = (256, 384)
 STRIDE = 1024
 F32 = jnp.float32
 BF16 = jnp.bfloat16
@@ -254,27 +254,29 @@
     begin, end = ((0, split), (counts[1], counts[2]), (split, counts[1]))[part]
     slots = pot.shape[1]
     base = begin * TURN // LANES * LANES
-    short = (end * TURN - base <= WINDOW) & (base + WINDOW <= slots)
+    fits = [(end * TURN - base <= size) & (base + size <= slots) for size in WINDOWS]
+    cases = [
+        (fits[0], base, WINDOWS[0]),
+        (jnp.logical_not(fits[0]) & fits[1], base, WINDOWS[1]),
+        (jnp.logical_not(fits[0]) & jnp.logical_not(fits[1]), 0, slots),
+    ]
 
     def list_copies(offset, size):
         return [
             pltpu.make_async_copy(
                 conn.at[pl.ds(pl.multiple_of(offset + j * STRIDE, LANES), size)],
-                lists[j].at[pl.ds(offset, size)],
+                lists[j].at[pl.ds(pl.multiple_of(offset, LANES), size)],
                 arrived.at[j],
             )
             for j in range(NPC)
         ]
 
-    @pl.when(short)
-    def _():
-        for copy in list_copies(pl.multiple_of(base, LANES), WINDOW):
-            copy.start()
-
-    @pl.when(jnp.logical_not(short))
-    def _():
-        for copy in list_copies(0, slots):
-            copy.start()
+    for chosen, offset, size in cases:
+
+        @pl.when(chosen & (end > begin))
+        def _():
+            for copy in list_copies(offset, size):
+                copy.start()
 
     if first:
         for fetch in fetches:
@@ -301,15 +303,12 @@
     if part == 1:
         src[padded : padded + ghost.shape[0], :] = ghost[...].astype(F32)
 
-    @pl.when(short)
-    def _():
-        for copy in list_copies(pl.multiple_of(base, LANES), WINDOW):
-            copy.wait()
-
-    @pl.when(jnp.logical_not(short))
-    def _():
-        for copy in list_copies(0, slots):
-            copy.wait()
+    for chosen, offset, size in cases:
+
+        @pl.when(chosen & (end > begin))
+        def _():
+            for copy in list_copies(offset, size):
+                copy.wait()
 
     sums = (sum_a, sum_b)
     sweep(
@@ -426,7 +425,7 @@
     same = (batched[:, :, None] == batched[:, None, :]) & (batched[:, :, None] >= 0)
     apart = ~jnp.eye(BATCH, dtype=bool)[None, :, :, None]
     repeated = jnp.any(same & apart).astype(jnp.int32)
-    counts = jnp.stack([turns // 2, turns, turns + late_turns, repeated, turns // 16])
+    counts = jnp.stack([turns // 2, turns, turns + late_turns, repeated, 0 * turns])
     return lists, moved[NPC:], jnp.pad(counts, (0, LANES - counts.shape[0]))
 
 
@@ -622,8 +621,7 @@
         )
 
     inverse = 1.0 / (node_count * lax.axis_size("dom"))
-    near_own, near_edge = lax.optimization_barrier((own, own_edge))
-    near = (project(two, near_own) + project(two_half, near_edge)) * inverse
+    near = (project(own, two) + project(own_edge, two_half)).T * inverse
     far = (project(other, own) + project(other_edge, own_edge)) * inverse
     lower = lax.axis_index("band") == 0
     pair = jnp.concatenate([jnp.where(lower, near, far), jnp.where(lower, far, near)], 0)

time: 357 us -> 366 us (1.025)
  starting transfers between devices: 52.1 us -> 67.8 us
  Pallas kernels: 258 us -> 251 us
  waiting for transfers between devices: 17.6 us -> 13.4 us
    ppermute x1, starting transfers between devices: 1.57 us -> 11 us  [local(): other = lax.ppermute(two, 'band', turned)]
    pallas_call x9, Pallas kernels: 245 us -> 238 us  [cells(): pl.pallas_call(functools.partial(cells_kernel, part, which, edge_count, p...]
    ppermute x1, waiting for transfers between devices: 6.06 us -> 0.53 us  [local(): other = lax.ppermute(two, 'band', turned)]
    ppermute x8, starting transfers between devices: 32.7 us -> 36.4 us  [swap(): return lax.ppermute(value, 'dom', pairs)]
  transfers between devices with their start and end apart: 17 -> 17, of which waited for: 8 -> 9; matrix products, arithmetic and copies ran while one was open for 4% -> 3% of each run, Pallas kernels for 58% -> 56%
where the time goes in v1:
time: 366 us; the launch traced here: 361 us
  Pallas kernels  251 us (69%)
  starting transfers between devices  67.8 us (19%)
  waiting for transfers between devices  13.4 us (4%)
  matrix products  10.8 us (3%)
  local copies, waits for them, and re-layouts  7.88 us (2%)
  other arithmetic  7.4 us (2%)
    pallas_call x9, Pallas kernels, cells(): pl.pallas_call(functools.partial(cells_kernel, part, which, edge_count, p...  238 us
    ppermute x8, starting transfers between devices, swap(): return lax.ppermute(value, 'dom', pairs)  36.4 us
    ppermute x6, starting transfers between devices, from_behind(): lax.ppermute(value, axis, [(source, source + steps) for source in range(i...  18.2 us
    pallas_call x1, Pallas kernels, local(): pl.pallas_call(functools.partial(start_kernel, edge_count, len(early)), o...  13 us
    ppermute x8, waiting for transfers between devices, swap(): return lax.ppermute(value, 'dom', pairs)  11.5 us
    ppermute x1, starting transfers between devices, local(): other = lax.ppermute(two, 'band', turned)  11 us
    dot_general x4, matrix products, project(): lax.dot_general(columns, mine, (((0,), (0,)), ((), ())), preferred_elemen...  7.85 us
  transfers between devices with their start and end apart: 17, of which 9 were waited for; matrix products, arithmetic and copies ran while one was open for 3% of the time, Pallas kernels for 56%

profile of v1, /device:TPU:0, one launch (start us, length us, event | category | flops | bytes accessed | tf_op | source)
XLA Modules:
  0.0 361.3 jit_solution(17991896497749299688)
XLA Ops:
  0.6 0.7 slice.57
  1.3 1.6 collective-permute-start
  2.9 0.9 compare_reduce_fusion
  3.9 0.6 convert_reduce_fusion.9
  5.1 1.0 fusion.20
  6.2 1.0 broadcast_compare_fusion
  8.4 0.9 pad_bitcast_fusion.1.mass_rows
  9.3 0.5 fusion.1
  10.1 1.7 fusion
  11.9 0.7 pad_maximum_fusion.4.refs_3_
  12.7 1.1 and_reduce_fusion
  14.0 0.8 copy.39
  15.5 0.7 pad.18.refs_0_
  16.3 2.2 copy-done.2
  18.5 13.0 %start.1 = (f32[16512,128]{1,0:T(8,128)}, bf16[16512,128]{1,0:T(8,128)(2,1)}, f32[1376,128]{1,0:T(8,128)S(1)}, f32[1376,128]{1,0:T(8,128)S(1)}, bf16[1376,128]{1...) custom-call(bf16[16428,128]{1,0:T(8,128)(2,1)S(1)} %copy-done.2, ...), custom_call_target="tpu_custom_call" | custom-call | flops 10000000000 | bytes 10000000 | tf_op jit(solution)/shard_map/start/pallas_call | solution.py:524
  31.5 1.3 collective-permute-start.1
  32.8 31.2 %cells_1_0.1 = (f32[17920,128]{1,0:T(8,128)S(1)}, f32[17920,128]{1,0:T(8,128)S(1)}, f32[17920,128]{1,0:T(8,128)S(1)}) custom-call(s32[65536]{0:T(1024)S(1)} %bitcast.27, s32[128]{0:T(128)S(4)} %get-tuple-element.48.refs_1_, f32[64,640]{1,0:T(8,128)S(1)} %get-tuple-element.49.refs_2_, bf16[128,64]{1,0:T(8,128)(2,1)S(1)} %get-tuple-element.50.refs_3_, ...), custom_call_target="tpu_custom_call" | custom-call | flops 20000000000 | bytes 20000000 | tf_op jit(solution)/shard_map/cells_1_0/pallas_call | solution.py:542
  64.1 17.4 %cells_1_1.1 = (f32[17920,128]{1,0:T(8,128)S(1)}, f32[17920,128]{1,0:T(8,128)S(1)}, f32[17920,128]{1,0:T(8,128)S(1)}, bf16[1376,128]{1,0:T(8,128)(2,1)S(1)}) custom-call(s32[65536]{0:T(1024)S(1)} %bitcast.28, s32[128]{0:T(128)S(4)} %get-tuple-element.48.refs_1_, ...), custom_call_target="tpu_custom_call", output_to_operand_aliasing={{0}: (5, {}), {1}: (6, {}), {2}: (7, {})} | custom-call | flops 20000000000 | bytes 20000000 | tf_op jit(solution)/shard_map/cells_1_1/pallas_call | solution.py:542
  81.5 3.1 collective-permute-start.2
  84.6 32.7 %cells_1_2.1 = (f32[17920,128]{1,0:T(8,128)S(1)}, f32[17920,128]{1,0:T(8,128)S(1)}, f32[17920,128]{1,0:T(8,128)S(1)}, f32[1376,128]{1,0:T(8,128)S(1)}, bf16[16512,128]{1,0:T(8,128)(2,1)}) custom-call(s32[65536]{0:T(1024)S(1)} %bitcast.29, s32[128]{0:T(128)S(4)} %get-tuple-element.48.refs_1_, ...), custom_call_target="tpu_custom_call", output_to_operand_aliasing={{0}: (5, {}), {1}: (6, {}), {2}: (7, {})} | custom-call | flops 20000000000 | bytes 20000000 | tf_op jit(solution)/shard_map/cells_1_2/pallas_call | solution.py:542
  117.5 1.3 collective-permute-start.3
  118.8 25.1 %cells_2_0.1 = (f32[17920,128]{1,0:T(8,128)S(1)}, f32[17920,128]{1,0:T(8,128)S(1)}, f32[17920,128]{1,0:T(8,128)S(1)}) custom-call(s32[65536]{0:T(1024)S(1)} %bitcast.30, s32[128]{0:T(128)S(4)} %get-tuple-element.48.refs_1_, f32[64,640]{1,0:T(8,128)S(1)} %get-tuple-element.49.refs_2_, ...), custom_call_target="tpu_custom_call", output_to_operand_aliasing={{0}: (5, {}), {1}: (6, {}), {2}: (7, {})} | custom-call | flops 20000000000 | bytes 20000000 | tf_op jit(solution)/shard_map/cells_2_0/pallas_call | solution.py:542
  143.9 17.4 %cells_2_1.1 = (f32[17920,128]{1,0:T(8,128)S(1)}, f32[17920,128]{1,0:T(8,128)S(1)}, f32[17920,128]{1,0:T(8,128)S(1)}, bf16[1376,128]{1,0:T(8,128)(2,1)S(1)}) custom-call(s32[65536]{0:T(1024)S(1)} %bitcast.31, s32[128]{0:T(128)S(4)} %get-tuple-element.48.refs_1_, ...), custom_call_target="tpu_custom_call", output_to_operand_aliasing={{0}: (5, {}), {1}: (6, {}), {2}: (7, {})} | custom-call | flops 20000000000 | bytes 20000000 | tf_op jit(solution)/shard_map/cells_2_1/pallas_call | solution.py:542
  161.3 4.1 %collective-permute-start.4 = (bf16[1376,128]{1,0:T(8,128)(2,1)S(1)}, bf16[1376,128]{1,0:T(8,128)(2,1)S(1)}, u32[]{:S(2)}, u32[]{:S(2)}) collective-permute-start(bf16[1376,128]{1,0:T(8,128)(2,1)S(1)} %get-tuple-element.80), channel_id=1, source_target_pairs={{0,2},{2,4},{4,6},{6,8},{8,10},{10,12},{12,14},{14,16},{16,18},{18... | collective-permute-start | bytes 1056776 | tf_op jit(solution)/shard_map/ppermute | solution.py:42
  165.4 32.9 %cells_2_2.1 = (f32[17920,128]{1,0:T(8,128)S(1)}, f32[17920,128]{1,0:T(8,128)S(1)}, f32[17920,128]{1,0:T(8,128)S(1)}, f32[1376,128]{1,0:T(8,128)S(1)}, bf16[16512,128]{1,0:T(8,128)(2,1)}) custom-call(s32[65536]{0:T(1024)S(1)} %bitcast.32, s32[128]{0:T(128)S(4)} %get-tuple-element.48.refs_1_, ...), custom_call_target="tpu_custom_call", output_to_operand_aliasing={{0}: (5, {}), {1}: (6, {}), {2}: (7, {})} | custom-call | flops 20000000000 | bytes 20000000 | tf_op jit(solution)/shard_map/cells_2_2/pallas_call | solution.py:542
  198.7 0.6 collective-permute-start.8
  199.3 1.3 collective-permute-start.5
  200.6 1.9 cells_3_0.1
  202.4 1.3 collective-permute-done.5.refs_8_
  203.8 11.0 %collective-permute-start.7 = (bf16[16512,128]{1,0:T(8,128)(2,1)}, bf16[16512,128]{1,0:T(8,128)(2,1)S(1)}, u32[]{:S(2)}, u32[]{:S(2)}) collective-permute-start(bf16[16512,128]{1,0:T(8,128)(2,1)} %get-tuple-element.89.refs_11_), channel_id=1, source_target_pairs={{0,1},{1,0},{2,3},{3,2},{4,5},{5,4},{6,7},{7,6},{8,9},{9,8},{10,11... | collective-permute-start | bytes 12681224 | tf_op jit(solution)/shard_map/ppermute | solution.py:603
  214.7 17.4 %cells_3_1.1 = (f32[17920,128]{1,0:T(8,128)S(1)}, f32[17920,128]{1,0:T(8,128)S(1)}, f32[17920,128]{1,0:T(8,128)S(1)}, bf16[1376,128]{1,0:T(8,128)(2,1)S(1)}) custom-call(s32[65536]{0:T(1024)S(1)} %bitcast.34, s32[128]{0:T(128)S(4)} %get-tuple-element.48.refs_1_, ...), custom_call_target="tpu_custom_call", output_to_operand_aliasing={{0}: (5, {}), {1}: (6, {}), {2}: (7, {})} | custom-call | flops 20000000000 | bytes 20000000 | tf_op jit(solution)/shard_map/cells_3_1/pallas_call | solution.py:542
  232.2 7.2 %collective-permute-start.6 = (bf16[1376,128]{1,0:T(8,128)(2,1)S(1)}, bf16[1376,128]{1,0:T(8,128)(2,1)S(1)}, u32[]{:S(2)}, u32[]{:S(2)}) collective-permute-start(bf16[1376,128]{1,0:T(8,128)(2,1)S(1)} %get-tuple-element.93), channel_id=1, source_target_pairs={{0,2},{2,4},{4,6},{6,8},{8,10},{10,12},{12,14},{14,16},{16,18},{18... | collective-permute-start | bytes 1056776 | tf_op jit(solution)/shard_map/ppermute | solution.py:42
  239.4 62.2 %cells_3_2.1 = (f32[17920,128]{1,0:T(8,128)S(1)}, f32[17920,128]{1,0:T(8,128)S(1)}, f32[17920,128]{1,0:T(8,128)S(1)}, f32[1376,128]{1,0:T(8,128)S(1)}, bf16[1651...) custom-call(s32[65536]{0:T(1024)S(1)} %bitcast.35, ...), custom_call_target="tpu_custom_call", output_to_operand_aliasing={{0}: (5, {}), {1}: (6, {}), {2}: (7, {})} | custom-call | flops 20000000000 | bytes 20000000 | tf_op jit(solution)/shard_map/cells_3_2/pallas_call | solution.py:542
  302.4 0.5 collective-permute-done.7
  302.9 5.7 %fusion.3 = f32[128,256]{1,0:T(8,128)S(1)} fusion(f32[128,256]{1,0:T(8,128)S(1)} %fusion.12, bf16[16512,128]{1,0:T(8,128)(2,1)S(1)} %collective-permute-done.7, bf16[16512,256]{1,0:T(8,128)(2,1)} %get-tuple-element.91), kind=kOutput, calls=%fused_computation.8 | convolution fusion | flops 1082195968 | bytes 12943360 | tf_op jit(solution)/shard_map/dot_general | solution.py:619
  309.1 1.5 broadcast_select_fusion.1
  311.8 3.9 %collective-permute-start.9 = (f32[32,2048]{1,0:T(8,128)S(1)}, f32[32,2048]{1,0:T(8,128)S(1)}, u32[]{:S(2)}, u32[]{:S(2)}) collective-permute-start(f32[32,2048]{1,0:T(8,128)S(1)} %reshape.584), channel_id=1, source_target_pairs={{0,2},{2,0},{4,6},{6,4},{8,10},{10,8},{12,14},{14,12},{16,18},{18,... | collective-permute-start | bytes 786440 | tf_op jit(solution)/shard_map/ppermute | solution.py:441
  315.7 1.2 collective-permute-done.9
  316.9 26.0 %collective-permute-start.10 = (bf16[32,2048]{1,0:T(8,128)(2,1)S(1)}, bf16[32,2048]{1,0:T(8,128)(2,1)S(1)}, u32[]{:S(2)}, u32[]{:S(2)}) collective-permute-start(bf16[32,2048]{1,0:T(8,128)(2,1)S(1)} %get-tuple-element.102), channel_id=1, source_target_pairs={{0,64},{2,66},{4,68},{6,70},{8,72},{10,74},{12,76},{14,78},{16,80}... | collective-permute-start | bytes 393224 | tf_op jit(solution)/shard_map/ppermute | solution.py:441
  342.8 3.8 %collective-permute-done.10 = bf16[32,2048]{1,0:T(8,128)(2,1)S(1)} collective-permute-done((bf16[32,2048]{1,0:T(8,128)(2,1)S(1)}, bf16[32,2048]{1,0:T(8,128)(2,1)S(1)}, u32[]{:S(2)}, u32[]{:S(2)}) %collective-permute-start.10) | collective-permute-done | bytes 131104 | tf_op jit(solution)/shard_map/ppermute | solution.py:441
  347.2 3.1 collective-permute-start.13
  350.3 3.0 collective-permute-done.11
  353.3 0.8 collective-permute-done.13
  354.5 0.5 collective-permute-start.15
  355.0 2.7 collective-permute-start.16
  357.7 1.7 collective-permute-done.14
  359.8 0.6 collective-permute-done.16
  360.5 0.7 reshape.585
  (99 shorter events, 5.9 us)
Async XLA Ops:
  0.6 6.6 %copy-start = (s32[8,8]{1,0:T(8,128)S(1)}, s32[8,8]{1,0:T(8,128)}, u32[]{:S(2)}) copy-start(s32[8,8]{1,0:T(8,128)} %param.15) | copy-start | bytes 772
  1.3 15.0 %collective-permute-start = (bf16[16,128]{1,0:T(8,128)(2,1)S(1)}, bf16[16,128]{1,0:T(8,128)(2,1)S(1)}, u32[]{:S(2)}, u32[]{:S(2)}) collective-permute-start(bf16[16,128]{1,0:T(8,128)(2,1)S(1)} %slice.57), channel_id=1, source_target_pairs={{0,1},{1,0},{2,3},{3,2},{4,5},{5,4},{6,7},{7,6},{8,9},{9,8},{10,11... | collective-permute-start | bytes 12296 | tf_op jit(solution)/shard_map/ppermute | solution.py:522
  8.0 7.4 %copy-start.3 = (pred[16,32]{1,0:T(8,128)(4,1)}, pred[16,32]{1,0:T(8,128)(4,1)S(1)}, u32[]{:S(2)}) copy-start(pred[16,32]{1,0:T(8,128)(4,1)S(1)} %fusion.40) | copy-start | bytes 1540
  8.1 23.4 %copy-start.5 = (pred[16,32]{1,0:T(8,128)(4,1)}, pred[16,32]{1,0:T(8,128)(4,1)S(1)}, u32[]{:S(2)}) copy-start(pred[16,32]{1,0:T(8,128)(4,1)S(1)} %fusion.41) | copy-start | bytes 1540
  8.2 23.3 %copy-start.7 = (pred[16,32]{1,0:T(8,128)(4,1)}, pred[16,32]{1,0:T(8,128)(4,1)S(1)}, u32[]{:S(2)}) copy-start(pred[16,32]{1,0:T(8,128)(4,1)S(1)} %fusion.42) | copy-start | bytes 1540
  8.3 23.2 %copy-start.9 = (pred[16,32]{1,0:T(8,128)(4,1)}, pred[16,32]{1,0:T(8,128)(4,1)S(1)}, u32[]{:S(2)}) copy-start(pred[16,32]{1,0:T(8,128)(4,1)S(1)} %fusion.43) | copy-start | bytes 1540
  16.3 2.2 copy-start.2
  31.5 32.6 %collective-permute-start.1 = (bf16[1376,128]{1,0:T(8,128)(2,1)S(1)}, bf16[1376,128]{1,0:T(8,128)(2,1)S(1)}, u32[]{:S(2)}, u32[]{:S(2)}) collective-permute-start(bf16[1376,128]{1,0:T(8,128)(2,1)S(1)} %get-tuple-element.57), channel_id=1, source_target_pairs={{2,0},{4,2},{6,4},{8,6},{10,8},{12,10},{14,12},{16,14},{18,16},{20... | collective-permute-start | bytes 1056776 | tf_op jit(solution)/shard_map/ppermute | solution.py:42
  81.5 35.8 %collective-permute-start.2 = (bf16[1376,128]{1,0:T(8,128)(2,1)S(1)}, bf16[1376,128]{1,0:T(8,128)(2,1)S(1)}, u32[]{:S(2)}, u32[]{:S(2)}) collective-permute-start(bf16[1376,128]{1,0:T(8,128)(2,1)S(1)} %get-tuple-element.67), channel_id=1, source_target_pairs={{0,2},{2,4},{4,6},{6,8},{8,10},{10,12},{12,14},{14,16},{16,18},{18... | collective-permute-start | bytes 1056776 | tf_op jit(solution)/shard_map/ppermute | solution.py:42
  117.5 26.4 %collective-permute-start.3 = (bf16[1376,128]{1,0:T(8,128)(2,1)S(1)}, bf16[1376,128]{1,0:T(8,128)(2,1)S(1)}, u32[]{:S(2)}, u32[]{:S(2)}) collective-permute-start(bf16[1376,128]{1,0:T(8,128)(2,1)S(1)} %get-tuple-element.109), channel_id=1, source_target_pairs={{2,0},{4,2},{6,4},{8,6},{10,8},{12,10},{14,12},{16,14},{18,16},{20... | collective-permute-start | bytes 1056776 | tf_op jit(solution)/shard_map/ppermute | solution.py:42
  161.3 37.0 %collective-permute-start.4 = (bf16[1376,128]{1,0:T(8,128)(2,1)S(1)}, bf16[1376,128]{1,0:T(8,128)(2,1)S(1)}, u32[]{:S(2)}, u32[]{:S(2)}) collective-permute-start(bf16[1376,128]{1,0:T(8,128)(2,1)S(1)} %get-tuple-element.80), channel_id=1, source_target_pairs={{0,2},{2,4},{4,6},{6,8},{8,10},{10,12},{12,14},{14,16},{16,18},{18... | collective-permute-start | bytes 1056776 | tf_op jit(solution)/shard_map/ppermute | solution.py:42
  198.7 103.4 %collective-permute-start.8 = (bf16[1376,128]{1,0:T(8,128)(2,1)S(1)}, bf16[1376,128]{1,0:T(8,128)(2,1)S(1)}, u32[]{:S(2)}, u32[]{:S(2)}) collective-permute-start(bf16[1376,128]{1,0:T(8,128)(2,1)S(1)} %get-tuple-element.105), channel_id=1, source_target_pairs={{0,1},{1,0},{2,3},{3,2},{4,5},{5,4},{6,7},{7,6},{8,9},{9,8},{10,11... | collective-permute-start | bytes 1056776 | tf_op jit(solution)/shard_map/ppermute | solution.py:597
  199.3 4.5 %collective-permute-start.5 = (bf16[1376,128]{1,0:T(8,128)(2,1)S(1)}, bf16[1376,128]{1,0:T(8,128)(2,1)S(1)}, u32[]{:S(2)}, u32[]{:S(2)}) collective-permute-start(bf16[1376,128]{1,0:T(8,128)(2,1)S(1)} %get-tuple-element.107), channel_id=1, source_target_pairs={{2,0},{4,2},{6,4},{8,6},{10,8},{12,10},{14,12},{16,14},{18,16},{20... | collective-permute-start | bytes 1056776 | tf_op jit(solution)/shard_map/ppermute | solution.py:42
  203.8 99.1 %collective-permute-start.7 = (bf16[16512,128]{1,0:T(8,128)(2,1)}, bf16[16512,128]{1,0:T(8,128)(2,1)S(1)}, u32[]{:S(2)}, u32[]{:S(2)}) collective-permute-start(bf16[16512,128]{1,0:T(8,128)(2,1)} %get-tuple-element.89.refs_11_), channel_id=1, source_target_pairs={{0,1},{1,0},{2,3},{3,2},{4,5},{5,4},{6,7},{7,6},{8,9},{9,8},{10,11... | collective-permute-start | bytes 12681224 | tf_op jit(solution)/shard_map/ppermute | solution.py:603
  232.2 69.4 %collective-permute-start.6 = (bf16[1376,128]{1,0:T(8,128)(2,1)S(1)}, bf16[1376,128]{1,0:T(8,128)(2,1)S(1)}, u32[]{:S(2)}, u32[]{:S(2)}) collective-permute-start(bf16[1376,128]{1,0:T(8,128)(2,1)S(1)} %get-tuple-element.93), channel_id=1, source_target_pairs={{0,2},{2,4},{4,6},{6,8},{8,10},{10,12},{12,14},{14,16},{16,18},{18... | collective-permute-start | bytes 1056776 | tf_op jit(solution)/shard_map/ppermute | solution.py:42
  301.7 6.9 %slice-start.3 = ((s8[4227072]{0:T(1024)(128)(4,1)}), s8[4194304]{0:T(1024)(128)(4,1)S(1)}, s32[]{:S(2)}) async-start(s8[4227072]{0:T(1024)(128)(4,1)} %bitcast.39), calls=%async_computation.3 | async-start | bytes 8388608
  302.1 6.6 %slice-start = ((s8[8454144]{0:T(1024)(128)(4,1)}), s8[4194304]{0:T(1024)(128)(4,1)S(1)}, s32[]{:S(2)}) async-start(s8[8454144]{0:T(1024)(128)(4,1)} %bitcast.37), calls=%async_computation | async-start | bytes 8388608
  302.9 6.1 %slice-start.1 = ((s8[8454144]{0:T(1024)(128)(4,1)}), s8[4194304]{0:T(1024)(128)(4,1)S(1)}, s32[]{:S(2)}) async-start(s8[8454144]{0:T(1024)(128)(4,1)} %bitcast.37), calls=%async_computation.1 | async-start | bytes 8388608
  302.9 6.1 %slice-start.2 = ((s8[8454144]{0:T(1024)(128)(4,1)}), s8[65536]{0:T(1024)(128)(4,1)S(1)}, s32[]{:S(2)}) async-start(s8[8454144]{0:T(1024)(128)(4,1)} %bitcast.37), calls=%async_computation.2 | async-start | bytes 131072
  302.9 6.1 %slice-start.4 = ((s8[4227072]{0:T(1024)(128)(4,1)}), s8[32768]{0:T(1024)(128)(4,1)S(1)}, s32[]{:S(2)}) async-start(s8[4227072]{0:T(1024)(128)(4,1)} %bitcast.39), calls=%async_computation.4 | async-start | bytes 65536
  309.0 37.6 %copy-start.4 = (pred[16,32]{1,0:T(8,128)(4,1)S(1)}, pred[16,32]{1,0:T(8,128)(4,1)}, u32[]{:S(2)}) copy-start(pred[16,32]{1,0:T(8,128)(4,1)} %copy-done.3) | copy-start | bytes 1540
  309.0 37.6 %copy-start.6 = (pred[16,32]{1,0:T(8,128)(4,1)S(1)}, pred[16,32]{1,0:T(8,128)(4,1)}, u32[]{:S(2)}) copy-start(pred[16,32]{1,0:T(8,128)(4,1)} %copy-done.5) | copy-start | bytes 1540
  309.0 37.6 %copy-start.8 = (pred[16,32]{1,0:T(8,128)(4,1)S(1)}, pred[16,32]{1,0:T(8,128)(4,1)}, u32[]{:S(2)}) copy-start(pred[16,32]{1,0:T(8,128)(4,1)} %copy-done.7) | copy-start | bytes 1540
  309.0 37.6 %copy-start.10 = (pred[16,32]{1,0:T(8,128)(4,1)S(1)}, pred[16,32]{1,0:T(8,128)(4,1)}, u32[]{:S(2)}) copy-start(pred[16,32]{1,0:T(8,128)(4,1)} %copy-done.9) | copy-start | bytes 1540
  309.1 52.1 %copy-start.1 = (s32[8,8]{1,0:T(8,128)S(1)}, s32[8,8]{1,0:T(8,128)}, u32[]{:S(2)}) copy-start(s32[8,8]{1,0:T(8,128)} %param.15) | copy-start | bytes 772
  311.8 5.0 %collective-permute-start.9 = (f32[32,2048]{1,0:T(8,128)S(1)}, f32[32,2048]{1,0:T(8,128)S(1)}, u32[]{:S(2)}, u32[]{:S(2)}) collective-permute-start(f32[32,2048]{1,0:T(8,128)S(1)} %reshape.584), channel_id=1, source_target_pairs={{0,2},{2,0},{4,6},{6,4},{8,10},{10,8},{12,14},{14,12},{16,18},{18,... | collective-permute-start | bytes 786440 | tf_op jit(solution)/shard_map/ppermute | solution.py:441
  316.9 29.8 %collective-permute-start.10 = (bf16[32,2048]{1,0:T(8,128)(2,1)S(1)}, bf16[32,2048]{1,0:T(8,128)(2,1)S(1)}, u32[]{:S(2)}, u32[]{:S(2)}) collective-permute-start(bf16[32,2048]{1,0:T(8,128)(2,1)S(1)} %get-tuple-element.102), channel_id=1, source_target_pairs={{0,64},{2,66},{4,68},{6,70},{8,72},{10,74},{12,76},{14,78},{16,80}... | collective-permute-start | bytes 393224 | tf_op jit(solution)/shard_map/ppermute | solution.py:441
  347.0 6.3 %collective-permute-start.11 = (bf16[16,2048]{1,0:T(8,128)(2,1)S(1)}, bf16[16,2048]{1,0:T(8,128)(2,1)S(1)}, u32[]{:S(2)}, u32[]{:S(2)}) collective-permute-start(bf16[16,2048]{1,0:T(8,128)(2,1)S(1)} %get-tuple-element.117), channel_id=1, source_target_pairs={{0,4},{2,6},{4,8},{6,10},{8,12},{10,14},{12,0},{14,2},{16,20},{18,... | collective-permute-start | bytes 196616 | tf_op jit(solution)/shard_map/ppermute | solution.py:441
  347.1 6.2 %collective-permute-start.12 = (bf16[16,2048]{1,0:T(8,128)(2,1)S(1)}, bf16[16,2048]{1,0:T(8,128)(2,1)S(1)}, u32[]{:S(2)}, u32[]{:S(2)}) collective-permute-start(bf16[16,2048]{1,0:T(8,128)(2,1)S(1)} %get-tuple-element.119), channel_id=1, source_target_pairs={{0,8},{2,10},{4,12},{6,14},{8,0},{10,2},{12,4},{14,6},{16,24},{18,... | collective-permute-start | bytes 196616 | tf_op jit(solution)/shard_map/ppermute | solution.py:441
  347.2 6.9 %collective-permute-start.13 = (bf16[16,2048]{1,0:T(8,128)(2,1)S(1)}, bf16[16,2048]{1,0:T(8,128)(2,1)S(1)}, u32[]{:S(2)}, u32[]{:S(2)}) collective-permute-start(bf16[16,2048]{1,0:T(8,128)(2,1)S(1)} %get-tuple-element.118), channel_id=1, source_target_pairs={{0,12},{2,14},{4,0},{6,2},{8,4},{10,6},{12,8},{14,10},{16,28},{18,... | collective-permute-start | bytes 196616 | tf_op jit(solution)/shard_map/ppermute | solution.py:441
  354.4 5.0 %collective-permute-start.14 = (bf16[4,2048]{1,0:T(4,128)(2,1)S(1)}, bf16[4,2048]{1,0:T(4,128)(2,1)S(1)}, u32[]{:S(2)}, u32[]{:S(2)}) collective-permute-start(bf16[4,2048]{1,0:T(4,128)(2,1)S(1)} %get-tuple-element.124), channel_id=1, source_target_pairs={{0,16},{2,18},{4,20},{6,22},{8,24},{10,26},{12,28},{14,30},{16,32}... | collective-permute-start | bytes 49160 | tf_op jit(solution)/shard_map/ppermute | solution.py:441
  354.5 5.3 %collective-permute-start.15 = (bf16[4,2048]{1,0:T(4,128)(2,1)S(1)}, bf16[4,2048]{1,0:T(4,128)(2,1)S(1)}, u32[]{:S(2)}, u32[]{:S(2)}) collective-permute-start(bf16[4,2048]{1,0:T(4,128)(2,1)S(1)} %get-tuple-element.126), channel_id=1, source_target_pairs={{0,32},{2,34},{4,36},{6,38},{8,40},{10,42},{12,44},{14,46},{16,48}... | collective-permute-start | bytes 49160 | tf_op jit(solution)/shard_map/ppermute | solution.py:441
  355.0 5.5 %collective-permute-start.16 = (bf16[4,2048]{1,0:T(4,128)(2,1)S(1)}, bf16[4,2048]{1,0:T(4,128)(2,1)S(1)}, u32[]{:S(2)}, u32[]{:S(2)}) collective-permute-start(bf16[4,2048]{1,0:T(4,128)(2,1)S(1)} %get-tuple-element.125), channel_id=1, source_target_pairs={{0,48},{2,50},{4,52},{6,54},{8,56},{10,58},{12,60},{14,62},{16,0},... | collective-permute-start | bytes 49160 | tf_op jit(solution)/shard_map/ppermute | solution.py:441
